TPU v7x, 32 devices: a whole 2x2x4 slice. The times are simulated.
32 devices in a mesh: grp: 2 (over y), pair: 4 (over z), aux: 2 (over x), occ: 2 (over core).
Axes of the slice: x: 2, y: 2, z: 4, core: 2. Of those that a mesh axis runs over, the one named last changes fastest.
Arguments:
- df_ints: bfloat16 [128, 4096, 256], P(('grp', 'pair'), ('aux', 'occ')), parts along dimension 0, may hold values from -2 to 2
- pno_rot: bfloat16 [64, 256, 256], P(('grp', 'pair')), parts along dimension 0, may hold values from -0.375 to 0.375
- margins: bfloat16 [64, 2, 256, 256], P(('grp', 'pair')), parts along dimension 0, may hold values from -0.375 to 0.375
- amplitudes: float32 [64, 256, 256], P(('grp', 'pair'), ('aux', 'occ')), parts along dimension 0, may hold values from -6 to 6
- virt_energy: float32 [64, 256], P(('grp', 'pair')), parts along dimension 0, may hold values from 0.5 to 4
- occ_gap: float32 [64], P(('grp', 'pair')), parts along dimension 0, may hold values from 0.5 to 2
- fock_coupling: float32 [64, 2], P(('grp', 'pair')), parts along dimension 0, may hold values from -3 to 3
- pno_count: int32 [64], P(('grp', 'pair')), parts along dimension 0, may hold values from 64 to 256, as said below
- pair_home: int32 [64, 2], P('grp'), parts along dimension 0, may hold values from 0 to 3, all different within a row; in each aligned block of 8 rows (0 to 7, 8 to 15, ...) at most 6 rows name the same one
- pair_slot: int32 [64, 2], P('grp'), parts along dimension 0, may hold values from 0 to 15
- neigh_home: int32 [64, 2], P('grp'), parts along dimension 0, may hold values from 0 to 3, all different within a row; in each aligned block of 8 rows (0 to 7, 8 to 15, ...) at most 6 rows name the same one
- neigh_slot: int32 [64, 2], P('grp'), parts along dimension 0, may hold values from 0 to 7
Outputs:
- new_amps: float32 [64, 256, 256], P(('grp', 'pair'), ('aux', 'occ')), parts along dimension 0
- pair_energy: float32 [64], P(('grp', 'pair')), parts along dimension 0
There are 2 independent parts, one for each index of `grp`. A program takes and returns all parts, laid end to end along the dimension named above; each array names one. Nothing has to cross between parts.
Inputs may be any that keep to these rules, and one draw needn't show every extreme that they name: `pair_home`: the two entries of a row differ. Among the rows of one owner's 8 pairs (aligned blocks), no value is named more than 6 times, and in some blocks one value is named exactly 6 times; every value is named somewhere. `neigh_home`: the entries of a row differ. Among the rows of one owner's 8 pairs (aligned blocks), no value is named more than 6 times, and in some blocks one value is named exactly 6 times; every value is named somewhere. `pno_count`: A multiple of one quarter of 256.
All inputs are finite; a program needn't handle non-finite values.
Results may differ from a plain program's by a relative error of at most 0.0018.
Values may be sent and summed in bfloat16 or wider, within the bound.
A program may use at most 128 MiB of HBM per device.

v0:
```python
import jax
import jax.numpy as jnp
from jax import lax
from jax.sharding import PartitionSpec as P


def routing(home_dev, slot_idx, table_rows, capacity, peer_count, own_index):
    requests = home_dev.reshape(peer_count, -1)
    slot_rows = slot_idx.reshape(peer_count, -1)
    peer_ids = jnp.arange(peer_count, dtype=jnp.int32)
    one_hot = (requests[:, :, None] == peer_ids[None, None, :]).astype(jnp.int32)
    slot_rank = jnp.sum((jnp.cumsum(one_hot, axis=1) - 1) * one_hot, axis=2)
    from_me = (requests == own_index).astype(jnp.int32)
    hit_slot = (
        slot_rank[:, :, None] == jnp.arange(capacity, dtype=jnp.int32)[None, None, :]
    ).astype(jnp.int32)
    hit_row = (
        slot_rows[:, :, None] == jnp.arange(table_rows, dtype=jnp.int32)[None, None, :]
    ).astype(jnp.int32)
    selector = jnp.sum(
        from_me[:, :, None, None] * hit_slot[:, :, :, None] * hit_row[:, :, None, :], axis=1
    )
    own_requests = lax.dynamic_index_in_dim(requests, own_index, 0, keepdims=False)
    own_rank = lax.dynamic_index_in_dim(slot_rank, own_index, 0, keepdims=False)
    position = own_requests * capacity + own_rank
    return (selector.astype(jnp.bfloat16), position)


def body(
    df_ints,
    pno_rot,
    margins,
    amplitudes,
    virt_energy,
    occ_gap,
    fock_coupling,
    pno_count,
    pair_home,
    pair_slot,
    neigh_home,
    neigh_slot,
):
    peer_count = lax.axis_size("pair")
    own_index = lax.axis_index("pair")
    group_index = lax.axis_index(("aux", "occ"))
    pairs_here = pno_rot.shape[0]
    pno_width = pno_rot.shape[1]
    capacity = 2 * pairs_here // peer_count + 2
    occ_rows = df_ints.shape[0]
    fit_rows = df_ints.shape[1]
    selector, position = routing(pair_home, pair_slot, occ_rows, capacity, peer_count, own_index)
    outgoing = jnp.einsum(
        "dct,tx->dcx", selector, df_ints.reshape(occ_rows, -1), preferred_element_type=jnp.float32
    ).astype(jnp.bfloat16)
    incoming = lax.all_to_all(outgoing, "pair", split_axis=0, concat_axis=0, tiled=True)
    blocks = jnp.take(
        incoming.reshape(peer_count * capacity, fit_rows, pno_width), position, axis=0
    )
    blocks = blocks.reshape(pairs_here, 2, fit_rows, pno_width)
    fitted = jnp.einsum(
        "peqv,pva->peqa", blocks, pno_rot, preferred_element_type=jnp.float32
    ).astype(jnp.bfloat16)
    exchange_part = jnp.einsum(
        "pqa,pqb->pab", fitted[:, 0], fitted[:, 1], preferred_element_type=jnp.float32
    )
    band_rows = amplitudes.shape[1]
    neigh_count = margins.shape[1]
    amp_wire = amplitudes.astype(jnp.bfloat16)
    selector_nb, position_nb = routing(
        neigh_home, neigh_slot, pairs_here, capacity, peer_count, own_index
    )
    outgoing_nb = jnp.einsum(
        "dct,tx->dcx",
        selector_nb,
        amp_wire.reshape(pairs_here, -1),
        preferred_element_type=jnp.float32,
    ).astype(jnp.bfloat16)
    incoming_nb = lax.all_to_all(outgoing_nb, "pair", split_axis=0, concat_axis=0, tiled=True)
    neighbour_band = jnp.take(
        incoming_nb.reshape(peer_count * capacity, band_rows, pno_width), position_nb, axis=0
    )
    neighbour_band = neighbour_band.reshape(pairs_here, neigh_count, band_rows, pno_width)
    row_start = group_index * band_rows
    margin_cols = lax.dynamic_slice_in_dim(margins, row_start, band_rows, axis=3)
    product_part = jnp.einsum(
        "pkar,pkrb->pkab", margin_cols, neighbour_band, preferred_element_type=jnp.float32
    )
    exchange_rows, projected_rows = (
        lax.psum_scatter(exchange_part, ("aux", "occ"), scatter_dimension=1, tiled=True),
        lax.psum_scatter(product_part, ("aux", "occ"), scatter_dimension=2, tiled=True),
    )
    projected = projected_rows.astype(jnp.bfloat16)
    coupled = jnp.einsum("pkrb,pkcb->pkrc", projected, margins, preferred_element_type=jnp.float32)
    coupling = jnp.sum(fock_coupling[:, :, None, None] * coupled, axis=1)
    energy_rows = lax.dynamic_slice_in_dim(virt_energy, row_start, band_rows, axis=1)
    denominator = energy_rows[:, :, None] + virt_energy[:, None, :] + occ_gap[:, None, None]
    residual = exchange_rows + denominator * amplitudes - coupling
    row_pos = row_start + jnp.arange(band_rows, dtype=jnp.int32)
    col_pos = jnp.arange(pno_width, dtype=jnp.int32)
    counts = pno_count[:, None, None]
    active = (row_pos[None, :, None] < counts) & (col_pos[None, None, :] < counts)
    updated = jnp.where(
        active, amplitudes - 0.5 * residual / denominator, jnp.zeros_like(amplitudes)
    )
    energy_part = jnp.sum(exchange_rows * updated, axis=(1, 2))
    pair_energy = lax.psum(energy_part, ("aux", "occ")) / pno_width
    return (updated, pair_energy)


def solution(mesh):
    placed = (
        P(("grp", "pair"), ("aux", "occ"), None),
        P(("grp", "pair"), None, None),
        P(("grp", "pair"), None, None, None),
        P(("grp", "pair"), ("aux", "occ"), None),
        P(("grp", "pair"), None),
        P(("grp", "pair")),
        P(("grp", "pair"), None),
        P(("grp", "pair")),
        P("grp", None),
        P("grp", None),
        P("grp", None),
        P("grp", None),
    )
    return jax.shard_map(
        body,
        mesh=mesh,
        in_specs=placed,
        out_specs=(P(("grp", "pair"), ("aux", "occ"), None), P(("grp", "pair"))),
        check_vma=False,
    )
```

profile of v0, /device:TPU:0, one launch (start us, length us, event | category | flops | bytes accessed | tf_op | source)
XLA Modules:
  0.0 508.0 jit_solution(11825827929969476050)
XLA Ops:
  7.2 0.9 copy.31
  8.1 0.1 reshape.222
  8.2 0.8 copy.26
  8.9 0.1 reshape.219
  9.0 1.1 convert_element_type.69
  10.1 0.1 reshape.243
  10.2 0.8 copy.32
  11.0 0.1 eq.135
  11.1 0.1 fusion.16
  11.2 0.2 select_reduce_fusion
  11.4 0.5 multiply_reduce_fusion.2
  11.9 1.4 convolution_convert_fusion.1
  13.3 6.3 %all-to-all-start.1 = ((bf16[4,6,16384]{2,1,0:T(8,128)(2,1)}), bf16[4,6,16384]{2,1,0:T(8,128)(2,1)S(1)}, u32[]{:S(2)}, u32[]{:S(2)}) async-start(bf16[4,6,16384]{2,1,0:T(8,128)(2,1)} %convolution_convert_fusion.1), calls=%async_computation.2 | async-start | bytes 2097152 | tf_op jit(solution)/shard_map/all_to_all | solution.py:78
  19.7 0.1 fusion.17
  19.7 8.0 %reshape.241 = bf16[16,262144,1]{1,0,2:T(8,128)(2,1)} reshape(bf16[16,1024,256]{2,1,0:T(8,128)(2,1)} %param.12) | data formatting | bytes 16777216 | tf_op jit(solution)/shard_map/reshape | solution.py:53
  27.7 0.1 copy.27
  27.8 0.1 eq.124
  27.9 0.1 fusion.18
  28.0 0.2 select_reduce_fusion.1
  28.2 0.1 multiply_reduce_fusion.1
  28.4 12.5 %convolution_convert_fusion = bf16[4,6,262144]{2,1,0:T(8,128)(2,1)} fusion(bf16[16,262144,1]{1,0,2:T(8,128)(2,1)} %reshape.241, s32[4,6,16]{2,1,0:T(8,128)S(1)} %multiply_reduce_fusion.1), kind=kOutput, calls=%fused_computation.2 | convolution fusion | flops 207618432 | bytes 20973056 | tf_op jit(solution)/shard_map/dct,tx->dcx/dot_general | solution.py:52
  40.9 4.5 all-to-all-done.1
  45.4 7.0 %all-to-all-start = ((bf16[4,6,262144]{2,1,0:T(8,128)(2,1)}), bf16[4,6,262144]{2,1,0:T(8,128)(2,1)}, u32[]{:S(2)}, u32[]{:S(2)}) async-start(bf16[4,6,262144]{2,1,0:T(8,128)(2,1)} %convolution_convert_fusion), calls=%async_computation | async-start | bytes 33554432 | tf_op jit(solution)/shard_map/all_to_all | solution.py:55
  52.4 0.0 reduce-scatter.5.cloned.1.call-start
  52.4 0.5 broadcast.242
  52.9 0.7 fusion.35
  53.6 0.1 add.143
  53.7 2.1 reshape.224
  55.8 1.7 gather_fusion.1
  57.6 2.8 fusion.10
  60.4 0.0 reduce-scatter.5.cloned.1.call-update
  60.4 0.2 reduce-scatter.3.cloned.1.call-start
  60.6 0.7 fusion.33
  61.3 0.1 add.131
  61.4 353.3 %all-to-all-done = bf16[4,6,262144]{2,1,0:T(8,128)(2,1)} async-done(((bf16[4,6,262144]{2,1,0:T(8,128)(2,1)}), bf16[4,6,262144]{2,1,0:T(8,128)(2,1)}, u32[]{:S(2)}, u32[]{:S(2)}) %all-to-all-start) | async-done | bytes 12582944 | tf_op jit(solution)/shard_map/all_to_all | solution.py:55
  414.7 22.5 %reshape.221 = bf16[24,1024,256]{2,1,0:T(8,128)(2,1)} reshape(bf16[4,6,262144]{2,1,0:T(8,128)(2,1)} %all-to-all-done) | data formatting | bytes 25165824 | tf_op jit(solution)/shard_map/reshape | solution.py:57
  437.3 9.4 %gather_fusion = bf16[16,1024,256]{2,1,0:T(8,128)(2,1)} fusion(bf16[24,1024,256]{2,1,0:T(8,128)(2,1)} %reshape.221, s32[1024]{0:T(1024)S(1)} %pad_clamp_fusion.1), kind=kCustom, calls=%fused_computation | custom fusion | bytes 16777280 | tf_op jit(solution)/shard_map/jit(_take)/gather | solution.py:56
  446.7 9.0 %fusion.3 = bf16[8,2,1024,256]{3,2,1,0:T(8,128)(2,1)} fusion(bf16[8,2,1024,256]{3,2,1,0:T(8,128)(2,1)} %bitcast.24, pred[8,2]{1,0:T(8,128)(4,1)S(1)} %compare_and_fusion.1, bf16[8,256,256]{2,1,0:T(8,128)(2,1)S(1)} %copy-done.7), kind=kOutput, calls=%fused_computation.7 | convolution fusion | flops 2155872256 | bytes 17825808 | tf_op jit(solution)/shard_map/peqv,pva->peqa/dot_general | solution.py:60
  455.7 6.3 %fusion.6 = f32[8,256,256]{2,1,0:T(8,128)} fusion(bf16[8,2,1024,256]{3,2,1,0:T(8,128)(2,1)} %fusion.3), kind=kOutput, calls=%fused_computation.9 | convolution fusion | flops 1073741824 | bytes 10485760 | tf_op jit(solution)/shard_map/pqa,pqb->pab/dot_general | solution.py:63
  462.0 0.1 copy.29
  462.1 0.1 constant_dynamic-slice_fusion.2
  462.2 0.1 broadcast_compare_fusion
  462.3 0.1 iota_compare_fusion.6
  462.3 2.0 fusion.8
  464.4 28.4 %reduce-scatter.3.cloned.1.call-done = f32[8,64,256]{2,1,0:T(8,128)} async-done(((f32[8,256,256]{2,1,0:T(8,128)}), f32[8,64,256]{2,1,0:T(8,128)}) %reduce-scatter.3.cloned.1.call-update) | async-done | bytes 524304 | tf_op jit(solution)/shard_map/reduce_scatter | solution.py:89
  492.8 2.2 multiply_reduce_fusion
  494.9 5.7 %psum.7 = f32[8]{0:T(128)S(1)} all-reduce(f32[8]{0:T(128)S(1)} %get-tuple-element.2), channel_id=1, replica_groups=mesh['grp'=2,'pair'=4,'aux'=2,'occ'=2] {'aux','occ'}, use_global_device_ids=true, to_apply=%region_10.11 | all-reduce | flops 8 | bytes 64 | tf_op jit(solution)/shard_map/psum | solution.py:106
  500.6 0.5 broadcast_multiply_fusion
  (31 shorter events, 0.2 us)
Async XLA Ops:
  7.2 50.4 %copy-start = (bf16[8,2,256,256]{3,2,1,0:T(8,128)(2,1)S(1)}, bf16[8,2,256,256]{3,2,1,0:T(8,128)(2,1)}, u32[]{:S(2)}) copy-start(bf16[8,2,256,256]{3,2,1,0:T(8,128)(2,1)} %param.14) | copy-start | bytes 6291460
  13.3 32.0 %all-to-all-start.1 = ((bf16[4,6,16384]{2,1,0:T(8,128)(2,1)}), bf16[4,6,16384]{2,1,0:T(8,128)(2,1)S(1)}, u32[]{:S(2)}, u32[]{:S(2)}) async-start(bf16[4,6,16384]{2,1,0:T(8,128)(2,1)} %convolution_convert_fusion.1), calls=%async_computation.2 | async-start | bytes 2097152 | tf_op jit(solution)/shard_map/all_to_all | solution.py:78
  19.7 8.0 %copy-start.4 = (s32[32,2]{0,1:T(2,128)S(1)}, s32[32,2]{0,1:T(2,128)}, u32[]{:S(2)}) copy-start(s32[32,2]{0,1:T(2,128)} %param.21) | copy-start | bytes 772
  45.4 369.3 %all-to-all-start = ((bf16[4,6,262144]{2,1,0:T(8,128)(2,1)}), bf16[4,6,262144]{2,1,0:T(8,128)(2,1)}, u32[]{:S(2)}, u32[]{:S(2)}) async-start(bf16[4,6,262144]{2,1,0:T(8,128)(2,1)} %convolution_convert_fusion), calls=%async_computation | async-start | bytes 33554432 | tf_op jit(solution)/shard_map/all_to_all | solution.py:55
  52.4 410.0 %reduce-scatter.5.cloned.1.call-start = ((), (), s32[]{:S(2)}) async-start(), calls=%async_computation.5 | async-start | bytes 5242880 | tf_op jit(solution)/shard_map/reduce_scatter | solution.py:90
  60.4 432.3 %reduce-scatter.3.cloned.1.call-start = ((), (), s32[]{:S(2)}) async-start(), calls=%async_computation.4 | async-start | bytes 2621440 | tf_op jit(solution)/shard_map/reduce_scatter | solution.py:89
  437.3 9.4 %copy-start.7 = (bf16[8,256,256]{2,1,0:T(8,128)(2,1)S(1)}, bf16[8,256,256]{2,1,0:T(8,128)(2,1)}, u32[]{:S(2)}) copy-start(bf16[8,256,256]{2,1,0:T(8,128)(2,1)} %param.13) | copy-start | bytes 3145732
  455.7 6.4 %copy-start.5 = (f32[8,2]{0,1:T(2,128)S(1)}, f32[8,2]{0,1:T(2,128)}, u32[]{:S(2)}) copy-start(f32[8,2]{0,1:T(2,128)} %param.18) | copy-start | bytes 196
  455.7 6.5 %copy-start.2 = (f32[8,256]{1,0:T(8,128)S(1)}, f32[8,256]{1,0:T(8,128)}, u32[]{:S(2)}) copy-start(f32[8,256]{1,0:T(8,128)} %param.16) | copy-start | bytes 24580
  455.7 6.5 %copy-start.3 = (s32[8]{0:T(128)S(1)}, s32[8]{0:T(128)}, u32[]{:S(2)}) copy-start(s32[8]{0:T(128)} %param.19) | copy-start | bytes 100
  455.7 37.1 %copy-start.1 = (f32[8,64,256]{2,1,0:T(8,128)S(1)}, f32[8,64,256]{2,1,0:T(8,128)}, u32[]{:S(2)}) copy-start(f32[8,64,256]{2,1,0:T(8,128)} %param.15) | copy-start | bytes 1572868
  455.7 37.1 %copy-start.6 = (f32[8]{0:T(128)S(1)}, f32[8]{0:T(128)}, u32[]{:S(2)}) copy-start(f32[8]{0:T(128)} %param.17) | copy-start | bytes 100
Sparse Core Ops, SparseCore 0:
  60.5 45.8 reduce-scatter.4
  462.1 30.5 reduce-scatter.2
where the time goes:
time: 509 us; the launch traced here: 508 us
  waiting for transfers between devices  386 us (76%)
  local copies, waits for them, and re-layouts  47.6 us (9%)
  matrix products  34.1 us (7%)
  between operations  14.2 us (3%)
  starting transfers between devices  13.5 us (3%)
  other arithmetic  6.66 us (1%)
  blocking collectives  5.73 us (1%)
    all_to_all x1, waiting for transfers between devices, body(): lax.all_to_all(outgoing, 'pair', split_axis=0, concat_axis=0, tiled=True)  353 us
    reduce_scatter x1, waiting for transfers between devices, body(): lax.psum_scatter(exchange_part, ('aux', 'occ'), scatter_dimension=1, tile...  28.4 us
    reshape x1, local copies, waits for them, and re-layouts, body(): incoming.reshape(peer_count * capacity, fit_rows, pno_width)  22.5 us
    dot_general x1, matrix products, body(): jnp.einsum('dct,tx->dcx', selector, df_ints.reshape(occ_rows, -1), prefer...  12.5 us
  transfers between devices with their start and end apart: 4, of which 3 were waited for; matrix products, arithmetic and copies ran while one was open for 16% of the time, Pallas kernels for 0%

commit v1 on v0

v1 whole, which is shorter than its diff:
```python
import jax
import jax.numpy as jnp
from jax import lax
from jax.sharding import PartitionSpec as P


def body(
    df_ints,
    pno_rot,
    margins,
    amplitudes,
    virt_energy,
    occ_gap,
    fock_coupling,
    pno_count,
    pair_home,
    pair_slot,
    neigh_home,
    neigh_slot,
):
    own_index = lax.axis_index("pair")
    group_index = lax.axis_index(("aux", "occ"))
    pairs_here, pno_width = pno_rot.shape[0], pno_rot.shape[1]
    occ_rows = df_ints.shape[0]
    band_rows = amplitudes.shape[1]
    neigh_count = margins.shape[1]
    orbital = pair_home * occ_rows + pair_slot
    own_homes = lax.dynamic_slice_in_dim(neigh_home, own_index * pairs_here, pairs_here, 0)
    own_slots = lax.dynamic_slice_in_dim(neigh_slot, own_index * pairs_here, pairs_here, 0)
    partner = own_homes * pairs_here + own_slots

    moved = lax.all_to_all(df_ints, "pair", split_axis=1, concat_axis=0, tiled=True)
    rot_all = lax.all_gather(pno_rot, "pair", axis=0, tiled=True)
    blocks = jnp.take(moved, orbital, axis=0)
    fitted = jnp.einsum(
        "peqv,pva->peqa", blocks, rot_all, preferred_element_type=jnp.float32
    ).astype(jnp.bfloat16)
    exchange_part = jnp.einsum(
        "pqa,pqb->pab", fitted[:, 0], fitted[:, 1], preferred_element_type=jnp.float32
    )
    exchange_mid = lax.psum_scatter(
        exchange_part, ("aux", "occ"), scatter_dimension=1, tiled=True
    )
    exchange_rows = lax.psum_scatter(exchange_mid, "pair", scatter_dimension=0, tiled=True)

    amp_all = lax.all_gather(amplitudes.astype(jnp.bfloat16), "pair", axis=0, tiled=True)
    picked = jnp.take(amp_all, partner, axis=0)
    neighbour = lax.all_gather(picked, ("aux", "occ"), axis=2, tiled=True)
    row_start = group_index * band_rows
    margin_rows = lax.dynamic_slice_in_dim(margins, row_start, band_rows, axis=2)
    projected = jnp.einsum(
        "pkrv,pkvb->pkrb", margin_rows, neighbour, preferred_element_type=jnp.float32
    ).astype(jnp.bfloat16)
    coupled = jnp.einsum("pkrb,pkcb->pkrc", projected, margins, preferred_element_type=jnp.float32)
    coupling = jnp.sum(fock_coupling[:, :, None, None] * coupled, axis=1)
    energy_rows = lax.dynamic_slice_in_dim(virt_energy, row_start, band_rows, axis=1)
    denominator = energy_rows[:, :, None] + virt_energy[:, None, :] + occ_gap[:, None, None]
    residual = exchange_rows + denominator * amplitudes - coupling
    row_pos = row_start + jnp.arange(band_rows, dtype=jnp.int32)
    col_pos = jnp.arange(pno_width, dtype=jnp.int32)
    counts = pno_count[:, None, None]
    active = (row_pos[None, :, None] < counts) & (col_pos[None, None, :] < counts)
    updated = jnp.where(
        active, amplitudes - 0.5 * residual / denominator, jnp.zeros_like(amplitudes)
    )
    energy_part = jnp.sum(exchange_rows * updated, axis=(1, 2))
    pair_energy = lax.psum(energy_part, ("aux", "occ")) / pno_width
    return (updated, pair_energy)


def solution(mesh):
    placed = (
        P(("grp", "pair"), ("aux", "occ"), None),
        P(("grp", "pair"), None, None),
        P(("grp", "pair"), None, None, None),
        P(("grp", "pair"), ("aux", "occ"), None),
        P(("grp", "pair"), None),
        P(("grp", "pair")),
        P(("grp", "pair"), None),
        P(("grp", "pair")),
        P("grp", None),
        P("grp", None),
        P("grp", None),
        P("grp", None),
    )
    return jax.shard_map(
        body,
        mesh=mesh,
        in_specs=placed,
        out_specs=(P(("grp", "pair"), ("aux", "occ"), None), P(("grp", "pair"))),
        check_vma=False,
    )
```

time: 509 us -> 489 us (0.961)
  waiting for transfers between devices: 386 us -> 402 us
  local copies, waits for them, and re-layouts: 47.6 us -> 33.5 us
  matrix products: 34.1 us -> 20.9 us
  starting transfers between devices: 13.5 us -> 6.8 us
    all_to_all x2 -> x1, waiting for transfers between devices: 358 us -> 266 us  [body(): lax.all_to_all(df_ints, 'pair', split_axis=1, concat_axis=0, tiled=True)]
    reduce_scatter x1, waiting for transfers between devices: 0.01 us -> 43.4 us  [body(): lax.psum_scatter(exchange_mid, 'pair', scatter_dimension=0, tiled=True)]
    reduce_scatter x1, waiting for transfers between devices: 28.4 us -> 67.2 us  [body(): lax.psum_scatter(exchange_part, ('aux', 'occ'), scatter_dimension=1, tile...]
    reshape x6 -> x0, local copies, waits for them, and re-layouts: 32.9 us -> none  [the longest x1 22.5 us: body(): incoming.reshape(peer_count * capacity, fit_rows, pno_width)]
    all_gather x0 -> x3, waiting for transfers between devices: none -> 24.3 us  [the longest x1 24.3 us: body(): neighbour = lax.all_gather(picked, ('aux', 'occ'), axis=2, tiled=True)]
    dot_general x4 -> x1, matrix products: 25.7 us -> 10.2 us  [body(): jnp.einsum('peqv,pva->peqa', blocks, rot_all, preferred_element_type=jnp....]
    all_to_all x0 -> x1, local copies, waits for them, and re-layouts: none -> 9.95 us  [body(): lax.all_to_all(df_ints, 'pair', split_axis=1, concat_axis=0, tiled=True)]
    unnamed x21 -> x22, local copies, waits for them, and re-layouts: 2.64 us -> 12.2 us
  transfers between devices with their start and end apart: 4 -> 6, of which waited for: 3 -> 4; matrix products, arithmetic and copies ran while one was open for 16% -> 9% of each run, Pallas kernels for 0% -> 0%
where the time goes in v1:
time: 489 us; the launch traced here: 488 us
  waiting for transfers between devices  402 us (82%)
  local copies, waits for them, and re-layouts  33.5 us (7%)
  matrix products  20.9 us (4%)
  between operations  13.9 us (3%)
  starting transfers between devices  6.8 us (1%)
  blocking collectives  6.37 us (1%)
    all_to_all x1, waiting for transfers between devices, body(): lax.all_to_all(df_ints, 'pair', split_axis=1, concat_axis=0, tiled=True)  266 us
    reduce_scatter x1, waiting for transfers between devices, body(): lax.psum_scatter(exchange_part, ('aux', 'occ'), scatter_dimension=1, tile...  67.2 us
    reduce_scatter x1, waiting for transfers between devices, body(): lax.psum_scatter(exchange_mid, 'pair', scatter_dimension=0, tiled=True)  43.4 us
    all_gather x1, waiting for transfers between devices, body(): neighbour = lax.all_gather(picked, ('aux', 'occ'), axis=2, tiled=True)  24.3 us
    unnamed x22, local copies, waits for them, and re-layouts  12.2 us
    dot_general x1, matrix products, body(): jnp.einsum('peqv,pva->peqa', blocks, rot_all, preferred_element_type=jnp....  10.2 us
    all_to_all x1, local copies, waits for them, and re-layouts, body(): lax.all_to_all(df_ints, 'pair', split_axis=1, concat_axis=0, tiled=True)  9.95 us
  transfers between devices with their start and end apart: 6, of which 4 were waited for; matrix products, arithmetic and copies ran while one was open for 9% of the time, Pallas kernels for 0%

profile of v1, /device:TPU:0, one launch (start us, length us, event | category | flops | bytes accessed | tf_op | source)
XLA Modules:
  0.0 488.1 jit_solution(822934633803005077)
XLA Ops:
  7.2 0.0 copy-start
  7.2 11.5 %copy.34 = bf16[16,1024,256]{2,0,1:T(8,128)(2,1)} copy(bf16[16,1024,256]{2,1,0:T(8,128)(2,1)} %param.12) | data formatting | bytes 16777216 | tf_op args[0]
  18.7 6.4 %all-to-all-start = ((bf16[16,1024,256]{2,0,1:T(8,128)(2,1)}), bf16[16,1024,256]{2,0,1:T(8,128)(2,1)}, u32[]{:S(2)}, u32[]{:S(2)}) async-start(bf16[16,1024,256]{2,0,1:T(8,128)(2,1)} %copy.34), calls=%async_computation | async-start | bytes 16777216 | tf_op jit(solution)/shard_map/all_to_all | solution.py:32
  25.2 0.0 all-gather.4.cloned.1.call-start
  25.2 0.7 all-gather.4.cloned.1.call-update
  25.9 0.0 all-gather.6.cloned.1.call-start
  25.9 0.0 copy-done.1
  26.0 0.7 convert_element_type.10
  26.7 0.0 all-gather.6.cloned.1.call-update
  26.7 0.2 reduce-scatter.3.cloned.1.call-start
  26.9 0.0 copy-done.4
  26.9 0.0 copy-done.5
  27.0 0.1 copy.37
  27.1 0.1 reshape.77
  27.2 0.1 copy.33
  27.3 266.3 %all-to-all-done = bf16[16,1024,256]{2,0,1:T(8,128)(2,1)} async-done(((bf16[16,1024,256]{2,0,1:T(8,128)(2,1)}), bf16[16,1024,256]{2,0,1:T(8,128)(2,1)}, u32[]{:S(2)}, u32[]{:S(2)}) %all-to-all-start) | async-done | bytes 8388640 | tf_op jit(solution)/shard_map/all_to_all | solution.py:32
  293.6 9.9 %copy.36 = bf16[4,16,256,256]{3,2,1,0:T(8,128)(2,1)} copy(bf16[4,16,256,256]{3,1,2,0:T(8,128)(2,1)} %bitcast.2) | data formatting | bytes 16777216 | tf_op jit(solution)/shard_map/all_to_all | solution.py:32
  303.5 8.9 %gather_fusion = bf16[64,256,256]{2,1,0:T(8,128)(2,1)} fusion(bf16[64,256,256]{2,1,0:T(8,128)(2,1)} %bitcast.19, s32[1024]{0:T(1024)S(1)} %pad_clamp_fusion.1), kind=kCustom, calls=%fused_computation | custom fusion | bytes 16777472 | tf_op jit(solution)/shard_map/jit(_take)/gather | solution.py:34
  312.4 10.2 %fusion.3 = bf16[32,2,256,256]{3,2,1,0:T(8,128)(2,1)} fusion(bf16[32,2,256,256]{3,2,1,0:T(8,128)(2,1)} %bitcast.20, pred[32,2]{1,0:T(8,128)(4,1)S(1)} %copy.33, bf16[32,256,256]{2,1,0:T(8,128)(2,1)} %all-gather.4.cloned.1.call-done), kind=kOutput, calls=%fused_computation.5 | convolution fusion | flops 2155872256 | bytes 20971584 | tf_op jit(solution)/shard_map/peqv,pva->peqa/dot_general | solution.py:35
  322.7 8.0 %fusion.6 = f32[32,256,256]{2,1,0:T(8,128)} fusion(bf16[32,2,256,256]{3,2,1,0:T(8,128)(2,1)} %fusion.3), kind=kOutput, calls=%fused_computation.7 | convolution fusion | flops 1073741824 | bytes 16777216 | tf_op jit(solution)/shard_map/pqa,pqb->pab/dot_general | solution.py:38
  330.7 0.0 copy-start.3
  330.7 0.0 copy-start.9
  330.7 0.0 reduce-scatter.3.cloned.1.call-update
  330.7 0.0 all-gather.8.cloned.1.call-start
  330.8 0.6 copy-done.7
  331.3 0.0 copy-done.8
  331.3 0.1 compare_and_fusion
  331.4 0.1 copy.41
  331.5 0.1 reshape.85
  331.6 0.1 copy.40
  331.7 0.0 all-gather.6.cloned.1.call-done
  331.7 1.8 gather_fusion.1
  333.5 0.9 broadcast_select_fusion
  334.4 0.0 all-gather.8.cloned.1.call-update
  334.5 0.0 reduce-scatter.5.cloned.1.call-start
  334.5 67.2 %reduce-scatter.3.cloned.1.call-done = f32[32,64,256]{2,1,0:T(8,128)} async-done(((f32[32,256,256]{2,1,0:T(8,128)}), f32[32,64,256]{2,1,0:T(8,128)}) %reduce-scatter.3.cloned.1.call-update) | async-done | bytes 2097168 | tf_op jit(solution)/shard_map/reduce_scatter | solution.py:41
  401.7 0.0 reduce-scatter.5.cloned.1.call-update
  401.7 0.0 copy-done.6
  401.7 0.1 copy.39
  401.8 0.1 constant_dynamic-slice_fusion
  401.9 0.1 broadcast_compare_fusion
  401.9 0.1 iota_compare_fusion
  402.0 24.3 %all-gather.8.cloned.1.call-done = bf16[8,2,256,256]{3,2,1,0:T(8,128)(2,1)} async-done(((bf16[8,2,64,256]{3,2,1,0:T(8,128)(2,1)}), bf16[8,2,256,256]{3,2,1,0:T(8,128)(2,1)}) %all-gather.8.cloned.1.call-update) | async-done | bytes 2097168 | tf_op jit(solution)/shard_map/all_gather | solution.py:48
  426.3 2.7 fusion.9
  429.1 43.4 %reduce-scatter.5.cloned.1.call-done = f32[8,64,256]{2,1,0:T(8,128)} async-done(((f32[32,64,256]{2,1,0:T(8,128)}), f32[8,64,256]{2,1,0:T(8,128)}) %reduce-scatter.5.cloned.1.call-update) | async-done | bytes 524304 | tf_op jit(solution)/shard_map/reduce_scatter | solution.py:44
  472.5 2.2 multiply_reduce_fusion
  474.7 6.4 %psum.7 = f32[8]{0:T(128)S(1)} all-reduce(f32[8]{0:T(128)S(1)} %get-tuple-element.2), channel_id=1, replica_groups=mesh['grp'=2,'pair'=4,'aux'=2,'occ'=2] {'aux','occ'}, use_global_device_ids=true, to_apply=%region_4.5 | all-reduce | flops 8 | bytes 64 | tf_op jit(solution)/shard_map/psum | solution.py:67
  481.0 0.5 broadcast_multiply_fusion
  (16 shorter events, 0.0 us)
Async XLA Ops:
  7.2 419.2 %copy-start = (bf16[8,2,256,256]{3,2,1,0:T(8,128)(2,1)S(1)}, bf16[8,2,256,256]{3,2,1,0:T(8,128)(2,1)}, u32[]{:S(2)}) copy-start(bf16[8,2,256,256]{3,2,1,0:T(8,128)(2,1)} %param.14) | copy-start | bytes 6291460
  18.7 7.2 %copy-start.1 = (f32[8,64,256]{2,1,0:T(8,128)S(1)}, f32[8,64,256]{2,1,0:T(8,128)}, u32[]{:S(2)}) copy-start(f32[8,64,256]{2,1,0:T(8,128)} %param.15) | copy-start | bytes 1572868
  18.7 8.2 %copy-start.4 = (s32[32,2]{0,1:T(2,128)S(1)}, s32[32,2]{0,1:T(2,128)}, u32[]{:S(2)}) copy-start(s32[32,2]{0,1:T(2,128)} %param.21) | copy-start | bytes 772
  18.7 8.2 %copy-start.5 = (s32[32,2]{0,1:T(2,128)S(1)}, s32[32,2]{0,1:T(2,128)}, u32[]{:S(2)}) copy-start(s32[32,2]{0,1:T(2,128)} %param.20) | copy-start | bytes 772
  18.7 274.9 %all-to-all-start = ((bf16[16,1024,256]{2,0,1:T(8,128)(2,1)}), bf16[16,1024,256]{2,0,1:T(8,128)(2,1)}, u32[]{:S(2)}, u32[]{:S(2)}) async-start(bf16[16,1024,256]{2,0,1:T(8,128)(2,1)} %copy.34), calls=%async_computation | async-start | bytes 16777216 | tf_op jit(solution)/shard_map/all_to_all | solution.py:32
  25.2 287.3 %all-gather.4.cloned.1.call-start = ((), (), s32[]{:S(2)}) async-start(), calls=%async_computation.3 | async-start | bytes 5242880 | tf_op jit(solution)/shard_map/all_gather | solution.py:33
  25.9 305.8 %all-gather.6.cloned.1.call-start = ((), (), s32[]{:S(2)}) async-start(), calls=%async_computation.6 | async-start | bytes 1310720 | tf_op jit(solution)/shard_map/all_gather | solution.py:46
  26.7 375.0 %reduce-scatter.3.cloned.1.call-start = ((), (), s32[]{:S(2)}) async-start(), calls=%async_computation.4 | async-start | bytes 10485760 | tf_op jit(solution)/shard_map/reduce_scatter | solution.py:41
  330.7 0.7 copy-start.7
  330.7 0.7 copy-start.8
  330.7 71.0 %copy-start.6 = (f32[8,2]{0,1:T(2,128)S(1)}, f32[8,2]{0,1:T(2,128)}, u32[]{:S(2)}) copy-start(f32[8,2]{0,1:T(2,128)} %param.18) | copy-start | bytes 196
  330.7 71.1 %copy-start.2 = (f32[8,256]{1,0:T(8,128)S(1)}, f32[8,256]{1,0:T(8,128)}, u32[]{:S(2)}) copy-start(f32[8,256]{1,0:T(8,128)} %param.16) | copy-start | bytes 24580
  330.7 71.2 %copy-start.3 = (s32[8]{0:T(128)S(1)}, s32[8]{0:T(128)}, u32[]{:S(2)}) copy-start(s32[8]{0:T(128)} %param.19) | copy-start | bytes 100
  330.7 141.8 %copy-start.9 = (f32[8]{0:T(128)S(1)}, f32[8]{0:T(128)}, u32[]{:S(2)}) copy-start(f32[8]{0:T(128)} %param.17) | copy-start | bytes 100
  330.7 95.6 %all-gather.8.cloned.1.call-start = ((), (), s32[]{:S(2)}) async-start(), calls=%async_computation.7 | async-start | bytes 2621440 | tf_op jit(solution)/shard_map/all_gather | solution.py:48
  334.5 138.0 %reduce-scatter.5.cloned.1.call-start = ((), (), s32[]{:S(2)}) async-start(), calls=%async_computation.5 | async-start | bytes 2621440 | tf_op jit(solution)/shard_map/reduce_scatter | solution.py:44
Sparse Core Ops, SparseCore 0:
  27.6 149.4 all-gather.3
  179.2 92.5 all-gather.5
  330.8 70.7 reduce-scatter.2
  403.7 22.5 all-gather.7
  428.6 43.8 reduce-scatter.4

commit v2 on v1

--- a/solution.py
+++ b/solution.py
@@ -1,7 +1,196 @@
+import functools
+
 import jax
 import jax.numpy as jnp
 from jax import lax
+from jax.experimental import pallas as pl
+from jax.experimental.pallas import tpu as pltpu
 from jax.sharding import PartitionSpec as P
+
+
+MESH = pl.DeviceIdType.MESH
+
+
+def exchange_kernel(
+    sizes, df, rot, idx, out,
+    dfb, rotb, ex, crecv, xsend, xrecv, zsend, zrecv,
+    local_sem, df_s, df_r, rz_s, rz_r, rg_s, rg_r, c_s, c_r, x_s, x_r, z_s, z_r,
+):
+    n_pair, n_aux, n_occ, pairs, share, occ_rows, depth = sizes
+    n_group = n_aux * n_occ
+    me, a, c = lax.axis_index("pair"), lax.axis_index("aux"), lax.axis_index("occ")
+    g = a * n_occ + c
+    other = 1 - c
+
+    def pair_peer(k):
+        return lax.rem(me + k, n_pair)
+
+    def group_peer(j):
+        peer = lax.rem(g + j, n_group)
+        return {"aux": peer // n_occ, "occ": lax.rem(peer, n_occ)}
+
+    def aux_peer(j):
+        return lax.rem(a + j, n_aux)
+
+    def remote(src, dst, send, recv, device):
+        return pltpu.make_async_remote_copy(
+            src_ref=src, dst_ref=dst, send_sem=send, recv_sem=recv,
+            device_id=device, device_id_type=MESH,
+        )
+
+    barrier = pltpu.get_barrier_semaphore()
+    for k in range(1, n_pair):
+        pl.semaphore_signal(barrier, inc=1, device_id={"pair": pair_peer(k)}, device_id_type=MESH)
+    for j in range(1, n_group):
+        pl.semaphore_signal(barrier, inc=1, device_id=group_peer(j), device_id_type=MESH)
+    pl.semaphore_wait(barrier, n_pair + n_group - 2)
+
+    own_df = pltpu.make_async_copy(
+        df.at[:, pl.ds(me * depth, depth), :], dfb.at[pl.ds(me * occ_rows, occ_rows)], local_sem.at[0]
+    )
+    own_rot = pltpu.make_async_copy(rot.at[g], rotb.at[me, g], local_sem.at[1])
+    own_rot.start()
+    rot_z = [
+        remote(rot.at[g], rotb.at[me, g], rz_s.at[k], rz_r.at[k], {"pair": pair_peer(k)})
+        for k in range(1, n_pair)
+    ]
+    for copy in rot_z:
+        copy.start()
+    moves = []
+    for k in range(1, n_pair):
+        peer = pair_peer(k)
+        moves.append(remote(
+            df.at[:, pl.ds(peer * depth, depth), :], dfb.at[pl.ds(me * occ_rows, occ_rows)],
+            df_s.at[k], df_r.at[k], {"pair": peer},
+        ))
+        moves[-1].start()
+    own_df.start()
+    own_rot.wait()
+    for copy in rot_z:
+        copy.wait()
+    rot_g = [
+        remote(rotb.at[:, g], rotb.at[:, g], rg_s.at[j], rg_r.at[j], group_peer(j))
+        for j in range(1, n_group)
+    ]
+    for copy in rot_g:
+        copy.start()
+    for copy in rot_g:
+        copy.wait()
+    own_df.wait()
+    for copy in moves:
+        copy.wait()
+
+    def owner_of(t):
+        return lax.rem(me + 1 + t, n_pair)
+
+    def core_copy(t):
+        return remote(
+            ex.at[t % 2, :, :, other], crecv.at[t], c_s.at[t], c_r.at[t], {"occ": other}
+        )
+
+    def aux_copy(t, j):
+        return remote(
+            xsend.at[t % 2, j - 1], xrecv.at[t, j - 1], x_s.at[t, j - 1], x_r.at[t, j - 1],
+            {"aux": aux_peer(j)},
+        )
+
+    def owner_copy(t):
+        return remote(zsend.at[t], zrecv.at[t], z_s.at[t], z_r.at[t], {"pair": owner_of(t)})
+
+    def contract(t):
+        owner = owner_of(t)
+
+        def one(p, carry):
+            row = (owner * pairs + p) * 2
+            left, right = dfb[idx[row]], dfb[idx[row + 1]]
+            turn = rotb[owner, p // share, lax.rem(p, share)]
+            left = jnp.dot(left, turn, preferred_element_type=jnp.float32).astype(jnp.bfloat16)
+            right = jnp.dot(right, turn, preferred_element_type=jnp.float32).astype(jnp.bfloat16)
+            both = lax.dot_general(
+                left, right, (((0,), (0,)), ((), ())), preferred_element_type=jnp.float32
+            )
+            ex[t % 2, p] = both.reshape(ex.shape[2:])
+            return carry
+
+        lax.fori_loop(0, pairs, one, 0)
+        core_copy(t).start()
+
+    def add_core(t):
+        core_copy(t).wait()
+        for j in range(1, n_aux):
+            peer = aux_peer(j)
+            xsend[t % 2, j - 1] = (ex[t % 2, :, peer, c] + crecv[t, :, peer]).astype(jnp.bfloat16)
+            aux_copy(t, j).start()
+        crecv[t, :, a] = crecv[t, :, a] + ex[t % 2, :, a, c]
+
+    def add_aux(t):
+        total = crecv[t, :, a]
+        for j in range(1, n_aux):
+            aux_copy(t, j).wait()
+            total = total + xrecv[t, j - 1].astype(jnp.float32)
+        if t < n_pair - 1:
+            zsend[t] = total.astype(jnp.bfloat16)
+            owner_copy(t).start()
+        else:
+            out[...] = total
+
+    for t in range(n_pair + 2):
+        if t < n_pair:
+            contract(t)
+        if 1 <= t < n_pair + 1:
+            add_core(t - 1)
+        if t >= 2:
+            add_aux(t - 2)
+    for t in range(n_pair - 1):
+        owner_copy(t).wait()
+        out[...] += zrecv[t].astype(jnp.float32)
+
+
+def exchange_sum(df_ints, pno_rot, orbital, band_rows):
+    n_pair, n_aux, n_occ = lax.axis_size("pair"), lax.axis_size("aux"), lax.axis_size("occ")
+    n_group = n_aux * n_occ
+    pairs, width = pno_rot.shape[0], pno_rot.shape[1]
+    share = pairs // n_group
+    occ_rows, fit_rows = df_ints.shape[0], df_ints.shape[1]
+    depth = fit_rows // n_pair
+    sizes = (n_pair, n_aux, n_occ, pairs, share, occ_rows, depth)
+    bf16, f32, dma = jnp.bfloat16, jnp.float32, pltpu.SemaphoreType.DMA
+    block = (pairs, band_rows, width)
+    others = max(1, n_aux - 1)
+    flops = 6 * n_pair * pairs * depth * width * width
+    return pl.pallas_call(
+        functools.partial(exchange_kernel, sizes),
+        out_shape=jax.ShapeDtypeStruct(block, f32),
+        in_specs=[
+            pl.BlockSpec(memory_space=pl.ANY),
+            pl.BlockSpec(memory_space=pl.ANY),
+            pl.BlockSpec(memory_space=pltpu.SMEM),
+        ],
+        out_specs=pl.BlockSpec(memory_space=pltpu.VMEM),
+        scratch_shapes=[
+            pltpu.VMEM((n_pair * occ_rows, depth, width), bf16),
+            pltpu.VMEM((n_pair, n_group, share, width, width), bf16),
+            pltpu.VMEM((2, pairs, n_aux, n_occ, band_rows, width), f32),
+            pltpu.VMEM((n_pair, pairs, n_aux, band_rows, width), f32),
+            pltpu.VMEM((2, others) + block, bf16),
+            pltpu.VMEM((n_pair, others) + block, bf16),
+            pltpu.VMEM((n_pair,) + block, bf16),
+            pltpu.VMEM((n_pair,) + block, bf16),
+            dma((2,)),
+            dma((n_pair,)), dma((n_pair,)),
+            dma((n_pair,)), dma((n_pair,)),
+            dma((n_group,)), dma((n_group,)),
+            dma((n_pair,)), dma((n_pair,)),
+            dma((n_pair, others)), dma((n_pair, others)),
+            dma((n_pair,)), dma((n_pair,)),
+        ],
+        compiler_params=pltpu.CompilerParams(
+            collective_id=0, has_side_effects=True, vmem_limit_bytes=58 << 20
+        ),
+        cost_estimate=pl.CostEstimate(
+            flops=flops, bytes_accessed=400 << 20, transcendentals=0
+        ),
+    )(df_ints, pno_rot.reshape(n_group, share, width, width), orbital.reshape(-1))
 
 
 def body(
@@ -29,19 +218,7 @@
     own_slots = lax.dynamic_slice_in_dim(neigh_slot, own_index * pairs_here, pairs_here, 0)
     partner = own_homes * pairs_here + own_slots
 
-    moved = lax.all_to_all(df_ints, "pair", split_axis=1, concat_axis=0, tiled=True)
-    rot_all = lax.all_gather(pno_rot, "pair", axis=0, tiled=True)
-    blocks = jnp.take(moved, orbital, axis=0)
-    fitted = jnp.einsum(
-        "peqv,pva->peqa", blocks, rot_all, preferred_element_type=jnp.float32
-    ).astype(jnp.bfloat16)
-    exchange_part = jnp.einsum(
-        "pqa,pqb->pab", fitted[:, 0], fitted[:, 1], preferred_element_type=jnp.float32
-    )
-    exchange_mid = lax.psum_scatter(
-        exchange_part, ("aux", "occ"), scatter_dimension=1, tiled=True
-    )
-    exchange_rows = lax.psum_scatter(exchange_mid, "pair", scatter_dimension=0, tiled=True)
+    exchange_rows = exchange_sum(df_ints, pno_rot, orbital, band_rows)
 
     amp_all = lax.all_gather(amplitudes.astype(jnp.bfloat16), "pair", axis=0, tiled=True)
     picked = jnp.take(amp_all, partner, axis=0)

time: 489 us -> 313 us (0.64)
  waiting for transfers between devices: 402 us -> 30.6 us
  Pallas kernels: 0 us -> 249 us
  local copies, waits for them, and re-layouts: 33.5 us -> 2.97 us
  matrix products: 20.9 us -> 2.78 us
  starting transfers between devices: 6.8 us -> 0.08 us
    all_to_all x1 -> x0, waiting for transfers between devices: 266 us -> none  [body(): lax.all_to_all(df_ints, 'pair', split_axis=1, concat_axis=0, tiled=True)]
    pallas_call x0 -> x1, Pallas kernels: none -> 249 us  [exchange_sum(): pl.pallas_call(functools.partial(exchange_kernel, sizes), out_shape=jax.S...]
    reduce_scatter x2 -> x0, waiting for transfers between devices: 111 us -> none  [the longest x1 67.2 us: body(): lax.psum_scatter(exchange_part, ('aux', 'occ'), scatter_dimension=1, tile...]
    all_gather x1, waiting for transfers between devices: 0.01 us -> 30.6 us  [body(): lax.all_gather(amplitudes.astype(jnp.bfloat16), 'pair', axis=0, tiled=True)]
    all_gather x1, waiting for transfers between devices: 24.3 us -> 0.02 us  [body(): neighbour = lax.all_gather(picked, ('aux', 'occ'), axis=2, tiled=True)]
    dot_general x2 -> x0, matrix products: 18.2 us -> none  [the longest x1 10.2 us: body(): jnp.einsum('peqv,pva->peqa', blocks, rot_all, preferred_element_type=jnp....]
    unnamed x22 -> x17, local copies, waits for them, and re-layouts: 12.2 us -> 0.12 us
    all_to_all x1 -> x0, local copies, waits for them, and re-layouts: 9.95 us -> none  [body(): lax.all_to_all(df_ints, 'pair', split_axis=1, concat_axis=0, tiled=True)]
  transfers between devices with their start and end apart: 6 -> 2, of which waited for: 4 -> 1; matrix products, arithmetic and copies ran while one was open for 9% -> 1% of each run, Pallas kernels for 0% -> 80%
where the time goes in v2:
time: 313 us; the launch traced here: 312 us
  Pallas kernels  249 us (80%)
  waiting for transfers between devices  30.6 us (10%)
  between operations  14.2 us (5%)
  other arithmetic  6.44 us (2%)
  blocking collectives  5.87 us (2%)
    pallas_call x1, Pallas kernels, exchange_sum(): pl.pallas_call(functools.partial(exchange_kernel, sizes), out_shape=jax.S...  249 us
    all_gather x1, waiting for transfers between devices, body(): lax.all_gather(amplitudes.astype(jnp.bfloat16), 'pair', axis=0, tiled=True)  30.6 us
  transfers between devices with their start and end apart: 2, of which 1 were waited for; matrix products, arithmetic and copies ran while one was open for 1% of the time, Pallas kernels for 80%

profile of v2, /device:TPU:0, one launch (start us, length us, event | category | flops | bytes accessed | tf_op | source)
XLA Modules:
  0.0 312.3 jit_solution(8446451248543777825)
XLA Ops:
  7.2 0.0 copy-start
  7.2 0.0 copy-start.4
  7.2 0.0 copy-start.6
  7.2 0.0 copy-start.5
  7.2 0.0 copy-start.2
  7.2 0.0 copy-start.3
  7.2 0.0 all-gather.3.cloned.1.call-start
  7.3 1.9 convert_element_type.6
  9.2 0.0 all-gather.3.cloned.1.call-update
  9.2 0.0 all-gather.5.cloned.1.call-start
  9.3 0.8 compare_and_fusion
  10.0 0.1 copy.25
  10.1 0.1 reshape.80
  10.2 0.1 copy.24
  10.3 30.6 %all-gather.3.cloned.1.call-done = bf16[32,64,256]{2,1,0:T(8,128)(2,1)} async-done(((bf16[8,64,256]{2,1,0:T(8,128)(2,1)}), bf16[32,64,256]{2,1,0:T(8,128)(2,1)}) %all-gather.3.cloned.1.call-update) | async-done | bytes 1048592 | tf_op jit(solution)/shard_map/all_gather | solution.py:223
  40.9 1.8 gather_fusion
  42.7 0.9 broadcast_select_fusion
  43.6 0.0 all-gather.5.cloned.1.call-update
  43.6 0.0 copy-done.4
  43.6 0.1 copy.23
  43.7 0.0 copy-done.6
  43.7 0.0 copy-done.5
  43.7 0.1 copy.22
  43.8 0.6 reshape.77.idx
  44.4 0.0 copy-done.2
  44.4 0.1 constant_dynamic-slice_fusion
  44.5 0.0 copy-done.3
  44.5 0.1 broadcast_compare_fusion
  44.6 0.1 iota_compare_fusion
  44.7 249.3 %shard_map.131 = f32[8,64,256]{2,1,0:T(8,128)} custom-call(bf16[16,1024,256]{2,1,0:T(8,128)(2,1)} %df.1, bf16[4,2,256,256]{3,2,1,0:T(8,128)(2,1)} %bitcast.5, s32[64]{0:T(128)} %reshape.77.idx), custom_call_target="tpu_custom_call" | custom-call | flops 3221225472 | bytes 419430400 | tf_op jit(solution)/shard_map/pallas_call | solution.py:161
  294.0 0.0 copy-start.1
  294.0 0.0 copy-start.7
  294.0 0.0 all-gather.5.cloned.1.call-done
  294.1 0.0 copy-done
  294.1 2.8 fusion
  296.8 0.0 copy-done.1
  296.9 0.0 copy-done.7
  296.9 2.2 multiply_reduce_fusion
  299.0 5.9 %psum.7 = f32[8]{0:T(128)S(1)} all-reduce(f32[8]{0:T(128)S(1)} %get-tuple-element.2), channel_id=1, replica_groups=mesh['grp'=2,'pair'=4,'aux'=2,'occ'=2] {'aux','occ'}, use_global_device_ids=true, to_apply=%region_2.3 | all-reduce | flops 8 | bytes 64 | tf_op jit(solution)/shard_map/psum | solution.py:244
  304.9 0.5 broadcast_multiply_fusion
  (3 shorter events, 0.0 us)
Async XLA Ops:
  7.2 286.9 %copy-start = (bf16[8,2,256,256]{3,2,1,0:T(8,128)(2,1)S(1)}, bf16[8,2,256,256]{3,2,1,0:T(8,128)(2,1)}, u32[]{:S(2)}) copy-start(bf16[8,2,256,256]{3,2,1,0:T(8,128)(2,1)} %param.14) | copy-start | bytes 6291460
  7.2 36.4 %copy-start.4 = (f32[8,2]{0,1:T(2,128)S(1)}, f32[8,2]{0,1:T(2,128)}, u32[]{:S(2)}) copy-start(f32[8,2]{0,1:T(2,128)} %param.18) | copy-start | bytes 196
  7.2 36.5 %copy-start.6 = (s32[32,2]{0,1:T(2,128)S(1)}, s32[32,2]{0,1:T(2,128)}, u32[]{:S(2)}) copy-start(s32[32,2]{0,1:T(2,128)} %param.20) | copy-start | bytes 772
  7.2 36.5 %copy-start.5 = (s32[32,2]{0,1:T(2,128)S(1)}, s32[32,2]{0,1:T(2,128)}, u32[]{:S(2)}) copy-start(s32[32,2]{0,1:T(2,128)} %param.21) | copy-start | bytes 772
  7.2 37.2 %copy-start.2 = (f32[8,256]{1,0:T(8,128)S(1)}, f32[8,256]{1,0:T(8,128)}, u32[]{:S(2)}) copy-start(f32[8,256]{1,0:T(8,128)} %param.16) | copy-start | bytes 24580
  7.2 37.3 %copy-start.3 = (s32[8]{0:T(128)S(1)}, s32[8]{0:T(128)}, u32[]{:S(2)}) copy-start(s32[8]{0:T(128)} %param.19) | copy-start | bytes 100
  7.2 33.6 %all-gather.3.cloned.1.call-start = ((), (), s32[]{:S(2)}) async-start(), calls=%async_computation | async-start | bytes 1310720 | tf_op jit(solution)/shard_map/all_gather | solution.py:223
  9.2 284.8 %all-gather.5.cloned.1.call-start = ((), (), s32[]{:S(2)}) async-start(), calls=%async_computation.1 | async-start | bytes 2621440 | tf_op jit(solution)/shard_map/all_gather | solution.py:225
  294.0 2.8 copy-start.1
  294.0 2.8 copy-start.7
Sparse Core Ops, SparseCore 0:
  10.2 30.6 all-gather.2
  43.7 22.1 all-gather.4

commit v3 on v2

--- a/solution.py
+++ b/solution.py
@@ -12,9 +12,10 @@
 
 
 def exchange_kernel(
-    sizes, df, rot, idx, out,
+    sizes, df, rot, idx, amp, out, amp_all,
     dfb, rotb, ex, crecv, xsend, xrecv, zsend, zrecv,
     local_sem, df_s, df_r, rz_s, rz_r, rg_s, rg_r, c_s, c_r, x_s, x_r, z_s, z_r,
+    az_s, az_r, ag_s, ag_r,
 ):
     n_pair, n_aux, n_occ, pairs, share, occ_rows, depth = sizes
     n_group = n_aux * n_occ
@@ -134,7 +135,26 @@
         else:
             out[...] = total
 
+    own_amp = pltpu.make_async_copy(amp, amp_all.at[me, g], local_sem.at[2])
+    own_amp.start()
+    amp_z = [
+        remote(amp, amp_all.at[me, g], az_s.at[k], az_r.at[k], {"pair": pair_peer(k)})
+        for k in range(1, n_pair)
+    ]
+    amp_g = [
+        remote(amp_all.at[:, g], amp_all.at[:, g], ag_s.at[j], ag_r.at[j], group_peer(j))
+        for j in range(1, n_group)
+    ]
+    for copy in amp_z:
+        copy.start()
+
     for t in range(n_pair + 2):
+        if t == n_pair - 1:
+            own_amp.wait()
+            for copy in amp_z:
+                copy.wait()
+            for copy in amp_g:
+                copy.start()
         if t < n_pair:
             contract(t)
         if 1 <= t < n_pair + 1:
@@ -144,9 +164,11 @@
     for t in range(n_pair - 1):
         owner_copy(t).wait()
         out[...] += zrecv[t].astype(jnp.float32)
-
-
-def exchange_sum(df_ints, pno_rot, orbital, band_rows):
+    for copy in amp_g:
+        copy.wait()
+
+
+def exchange_sum(df_ints, pno_rot, orbital, amp_wire):
     n_pair, n_aux, n_occ = lax.axis_size("pair"), lax.axis_size("aux"), lax.axis_size("occ")
     n_group = n_aux * n_occ
     pairs, width = pno_rot.shape[0], pno_rot.shape[1]
@@ -155,18 +177,26 @@
     depth = fit_rows // n_pair
     sizes = (n_pair, n_aux, n_occ, pairs, share, occ_rows, depth)
     bf16, f32, dma = jnp.bfloat16, jnp.float32, pltpu.SemaphoreType.DMA
-    block = (pairs, band_rows, width)
+    block = amp_wire.shape
+    band_rows = block[1]
     others = max(1, n_aux - 1)
     flops = 6 * n_pair * pairs * depth * width * width
     return pl.pallas_call(
         functools.partial(exchange_kernel, sizes),
-        out_shape=jax.ShapeDtypeStruct(block, f32),
+        out_shape=(
+            jax.ShapeDtypeStruct(block, f32),
+            jax.ShapeDtypeStruct((n_pair, n_group) + block, bf16),
+        ),
         in_specs=[
             pl.BlockSpec(memory_space=pl.ANY),
             pl.BlockSpec(memory_space=pl.ANY),
             pl.BlockSpec(memory_space=pltpu.SMEM),
+            pl.BlockSpec(memory_space=pl.ANY),
         ],
-        out_specs=pl.BlockSpec(memory_space=pltpu.VMEM),
+        out_specs=(
+            pl.BlockSpec(memory_space=pltpu.VMEM),
+            pl.BlockSpec(memory_space=pl.ANY),
+        ),
         scratch_shapes=[
             pltpu.VMEM((n_pair * occ_rows, depth, width), bf16),
             pltpu.VMEM((n_pair, n_group, share, width, width), bf16),
@@ -176,13 +206,15 @@
             pltpu.VMEM((n_pair, others) + block, bf16),
             pltpu.VMEM((n_pair,) + block, bf16),
             pltpu.VMEM((n_pair,) + block, bf16),
-            dma((2,)),
+            dma((3,)),
             dma((n_pair,)), dma((n_pair,)),
             dma((n_pair,)), dma((n_pair,)),
             dma((n_group,)), dma((n_group,)),
             dma((n_pair,)), dma((n_pair,)),
             dma((n_pair, others)), dma((n_pair, others)),
             dma((n_pair,)), dma((n_pair,)),
+            dma((n_pair,)), dma((n_pair,)),
+            dma((n_group,)), dma((n_group,)),
         ],
         compiler_params=pltpu.CompilerParams(
             collective_id=0, has_side_effects=True, vmem_limit_bytes=58 << 20
@@ -190,7 +222,7 @@
         cost_estimate=pl.CostEstimate(
             flops=flops, bytes_accessed=400 << 20, transcendentals=0
         ),
-    )(df_ints, pno_rot.reshape(n_group, share, width, width), orbital.reshape(-1))
+    )(df_ints, pno_rot.reshape(n_group, share, width, width), orbital.reshape(-1), amp_wire)
 
 
 def body(
@@ -216,13 +248,13 @@
     orbital = pair_home * occ_rows + pair_slot
     own_homes = lax.dynamic_slice_in_dim(neigh_home, own_index * pairs_here, pairs_here, 0)
     own_slots = lax.dynamic_slice_in_dim(neigh_slot, own_index * pairs_here, pairs_here, 0)
-    partner = own_homes * pairs_here + own_slots
-
-    exchange_rows = exchange_sum(df_ints, pno_rot, orbital, band_rows)
-
-    amp_all = lax.all_gather(amplitudes.astype(jnp.bfloat16), "pair", axis=0, tiled=True)
-    picked = jnp.take(amp_all, partner, axis=0)
-    neighbour = lax.all_gather(picked, ("aux", "occ"), axis=2, tiled=True)
+
+    exchange_rows, amp_all = exchange_sum(
+        df_ints, pno_rot, orbital, amplitudes.astype(jnp.bfloat16)
+    )
+    neighbour = amp_all[own_homes, :, own_slots].reshape(
+        pairs_here, neigh_count, pno_width, pno_width
+    )
     row_start = group_index * band_rows
     margin_rows = lax.dynamic_slice_in_dim(margins, row_start, band_rows, axis=2)
     projected = jnp.einsum(

time: 313 us -> 319 us (1.019)
  Pallas kernels: 249 us -> 298 us
  waiting for transfers between devices: 30.6 us -> 0 us
  between operations: 14.2 us -> 0.7 us
    pallas_call x1, Pallas kernels: 249 us -> 298 us  [exchange_sum(): pl.pallas_call(functools.partial(exchange_kernel, sizes), out_shape=(jax....]
    all_gather x2 -> x0, waiting for transfers between devices: 30.6 us -> none  [the longest x1 30.6 us: body(): lax.all_gather(amplitudes.astype(jnp.bfloat16), 'pair', axis=0, tiled=True)]
  transfers between devices with their start and end apart: 2 -> 0, of which waited for: 1 -> 0; matrix products, arithmetic and copies ran while one was open for 1% -> 0% of each run, Pallas kernels for 80% -> 0%
where the time goes in v3:
time: 319 us
  Pallas kernels  298 us (93%)
  blocking collectives  5.88 us (2%)
  other arithmetic  5.53 us (2%)
  local copies, waits for them, and re-layouts  5.28 us (2%)
    pallas_call x1, Pallas kernels, exchange_sum(): pl.pallas_call(functools.partial(exchange_kernel, sizes), out_shape=(jax....  298 us

profile of v3, /device:TPU:0, one launch (start us, length us, event | category | flops | bytes accessed | tf_op | source)
XLA Modules:
  0.0 318.7 jit_solution(10877904294057105183)
XLA Ops:
  0.6 0.0 copy-start
  0.6 0.8 multiply_add_fusion
  1.5 0.1 copy.17
  1.6 0.6 reshape.75.idx
  2.2 1.8 convert_element_type.6.amp
  4.0 0.0 copy-start.4
  4.0 0.0 copy-start.5
  4.0 298.5 %shard_map.131 = (f32[8,64,256]{2,1,0:T(8,128)}, bf16[4,4,8,64,256]{4,3,2,1,0:T(8,128)(2,1)}) custom-call(bf16[16,1024,256]{2,1,0:T(8,128)(2,1)} %df.1, bf16[4,2,256,256]{3,2,1,0:T(8,128)(2,1)} %bitcast.5, s32[64]{0:T(128)} %reshape.75.idx, bf16[8,64,256]{2,1,0:T(8,128)(2,1)} %convert_element_type.6.amp), custom_call_target="tpu_custom_call" | custom-call | flops 3221225472 | bytes 419430400 | tf_op jit(solution)/shard_map/pallas_call | solution.py:184
  302.5 0.0 copy-done.4
  302.5 0.0 copy-done.5
  302.5 0.1 fusion.5
  302.6 0.1 copy.19
  302.7 0.1 reshape.77
  302.7 0.0 copy-start.6
  302.7 4.2 %gather_fusion = bf16[16,4,64,256]{3,2,1,0:T(8,128)(2,1)} fusion(bf16[4,4,8,64,256]{4,3,2,1,0:T(8,128)(2,1)} %get-tuple-element.5, s32[16]{0:T(128)S(1)} %reshape.77), kind=kCustom, calls=%fused_computation | custom fusion | bytes 4194432 | tf_op jit(solution)/shard_map/gather | solution.py:255
  307.0 0.0 copy-done.6
  307.0 0.1 copy.18
  307.0 0.0 copy-done
  307.0 0.0 copy-start.2
  307.0 0.0 copy-start.3
  307.0 0.0 copy-start.1
  307.0 0.0 copy-start.7
  307.1 2.8 fusion
  309.8 0.0 copy-done.2
  309.9 0.1 constant_dynamic-slice_fusion
  309.9 0.0 copy-done.3
  309.9 0.1 iota_compare_fusion
  310.0 0.1 broadcast_compare_fusion
  310.1 0.0 copy-done.1
  310.1 0.0 copy-done.7
  310.1 2.2 multiply_reduce_fusion
  312.3 5.9 %psum.7 = f32[8]{0:T(128)S(1)} all-reduce(f32[8]{0:T(128)S(1)} %get-tuple-element.6), channel_id=1, replica_groups=mesh['grp'=2,'pair'=4,'aux'=2,'occ'=2] {'aux','occ'}, use_global_device_ids=true, to_apply=%region_2.3 | all-reduce | flops 8 | bytes 64 | tf_op jit(solution)/shard_map/psum | solution.py:276
  318.1 0.5 broadcast_multiply_fusion
  (1 shorter events, 0.0 us)
Async XLA Ops:
  0.6 306.4 %copy-start = (bf16[8,2,256,256]{3,2,1,0:T(8,128)(2,1)S(1)}, bf16[8,2,256,256]{3,2,1,0:T(8,128)(2,1)}, u32[]{:S(2)}) copy-start(bf16[8,2,256,256]{3,2,1,0:T(8,128)(2,1)} %param.14) | copy-start | bytes 6291460
  4.0 298.5 %copy-start.4 = (s32[32,2]{0,1:T(2,128)S(1)}, s32[32,2]{0,1:T(2,128)}, u32[]{:S(2)}) copy-start(s32[32,2]{0,1:T(2,128)} %param.23) | copy-start | bytes 772
  4.0 298.5 %copy-start.5 = (s32[32,2]{0,1:T(2,128)S(1)}, s32[32,2]{0,1:T(2,128)}, u32[]{:S(2)}) copy-start(s32[32,2]{0,1:T(2,128)} %param.22) | copy-start | bytes 772
  302.7 4.2 %copy-start.6 = (f32[8,2]{0,1:T(2,128)S(1)}, f32[8,2]{0,1:T(2,128)}, u32[]{:S(2)}) copy-start(f32[8,2]{0,1:T(2,128)} %param.18) | copy-start | bytes 196
  307.0 2.8 copy-start.2
  307.0 2.9 copy-start.3
  307.0 3.0 copy-start.1
  307.0 3.0 copy-start.7

commit v4 on v3

--- a/solution.py
+++ b/solution.py
@@ -50,12 +50,26 @@
         df.at[:, pl.ds(me * depth, depth), :], dfb.at[pl.ds(me * occ_rows, occ_rows)], local_sem.at[0]
     )
     own_rot = pltpu.make_async_copy(rot.at[g], rotb.at[me, g], local_sem.at[1])
+    own_amp = pltpu.make_async_copy(amp, amp_all.at[me, g], local_sem.at[2])
     own_rot.start()
-    rot_z = [
-        remote(rot.at[g], rotb.at[me, g], rz_s.at[k], rz_r.at[k], {"pair": pair_peer(k)})
-        for k in range(1, n_pair)
-    ]
-    for copy in rot_z:
+    own_amp.start()
+    own_rot.wait()
+    own_amp.wait()
+
+    def doubling(far):
+        near = far * 2
+        peer = me + far * (1 - 2 * lax.rem(me // far, 2))
+        copies = []
+        for i in range(n_pair // near):
+            block, sem = lax.rem(me, near) + near * i, n_pair // near + i
+            for table, send, recv in ((rotb, rz_s, rz_r), (amp_all, az_s, az_r)):
+                ref = table.at[block, g]
+                copies.append(remote(ref, ref, send.at[sem], recv.at[sem], {"pair": peer}))
+        return copies
+
+    hops = [n_pair >> (b + 1) for b in range(n_pair.bit_length() - 1)]
+    flying = doubling(hops[0])
+    for copy in flying:
         copy.start()
     moves = []
     for k in range(1, n_pair):
@@ -66,16 +80,25 @@
         ))
         moves[-1].start()
     own_df.start()
-    own_rot.wait()
-    for copy in rot_z:
+    for hop in hops[1:]:
+        for copy in flying:
+            copy.wait()
+        flying = doubling(hop)
+        for copy in flying:
+            copy.start()
+    for copy in flying:
         copy.wait()
     rot_g = [
         remote(rotb.at[:, g], rotb.at[:, g], rg_s.at[j], rg_r.at[j], group_peer(j))
         for j in range(1, n_group)
     ]
-    for copy in rot_g:
+    amp_g = [
+        remote(amp_all.at[:, g], amp_all.at[:, g], ag_s.at[j], ag_r.at[j], group_peer(j))
+        for j in range(1, n_group)
+    ]
+    for copy in rot_g + amp_g:
         copy.start()
-    for copy in rot_g:
+    for copy in rot_g + amp_g:
         copy.wait()
     own_df.wait()
     for copy in moves:
@@ -135,26 +158,7 @@
         else:
             out[...] = total
 
-    own_amp = pltpu.make_async_copy(amp, amp_all.at[me, g], local_sem.at[2])
-    own_amp.start()
-    amp_z = [
-        remote(amp, amp_all.at[me, g], az_s.at[k], az_r.at[k], {"pair": pair_peer(k)})
-        for k in range(1, n_pair)
-    ]
-    amp_g = [
-        remote(amp_all.at[:, g], amp_all.at[:, g], ag_s.at[j], ag_r.at[j], group_peer(j))
-        for j in range(1, n_group)
-    ]
-    for copy in amp_z:
-        copy.start()
-
     for t in range(n_pair + 2):
-        if t == n_pair - 1:
-            own_amp.wait()
-            for copy in amp_z:
-                copy.wait()
-            for copy in amp_g:
-                copy.start()
         if t < n_pair:
             contract(t)
         if 1 <= t < n_pair + 1:
@@ -164,8 +168,6 @@
     for t in range(n_pair - 1):
         owner_copy(t).wait()
         out[...] += zrecv[t].astype(jnp.float32)
-    for copy in amp_g:
-        copy.wait()
 
 
 def exchange_sum(df_ints, pno_rot, orbital, amp_wire):

time: 319 us -> 382 us (1.20)
  Pallas kernels: 298 us -> 359 us
    pallas_call x1, Pallas kernels: 298 us -> 359 us  [exchange_sum(): pl.pallas_call(functools.partial(exchange_kernel, sizes), out_shape=(jax....]
where the time goes in v4:
time: 382 us; the launch traced here: 379 us
  Pallas kernels  359 us (94%)
  blocking collectives  5.97 us (2%)
  other arithmetic  5.53 us (1%)
  local copies, waits for them, and re-layouts  5.28 us (1%)
    pallas_call x1, Pallas kernels, exchange_sum(): pl.pallas_call(functools.partial(exchange_kernel, sizes), out_shape=(jax....  359 us

profile of v4, /device:TPU:0, one launch (start us, length us, event | category | flops | bytes accessed | tf_op | source)
XLA Modules:
  0.0 378.9 jit_solution(10690323809253348444)
XLA Ops:
  0.6 0.0 copy-start
  0.6 0.8 multiply_add_fusion
  1.5 0.1 copy.17
  1.6 0.6 reshape.75.idx
  2.2 1.8 convert_element_type.6.amp
  4.0 0.0 copy-start.4
  4.0 0.0 copy-start.5
  4.0 358.6 %shard_map.131 = (f32[8,64,256]{2,1,0:T(8,128)}, bf16[4,4,8,64,256]{4,3,2,1,0:T(8,128)(2,1)}) custom-call(bf16[16,1024,256]{2,1,0:T(8,128)(2,1)} %df.1, bf16[4,2,256,256]{3,2,1,0:T(8,128)(2,1)} %bitcast.5, s32[64]{0:T(128)} %reshape.75.idx, bf16[8,64,256]{2,1,0:T(8,128)(2,1)} %convert_element_type.6.amp), custom_call_target="tpu_custom_call" | custom-call | flops 3221225472 | bytes 419430400 | tf_op jit(solution)/shard_map/pallas_call | solution.py:186
  362.6 0.0 copy-done.4
  362.6 0.0 copy-done.5
  362.6 0.1 fusion.5
  362.7 0.1 copy.19
  362.8 0.1 reshape.77
  362.9 0.0 copy-start.6
  362.9 4.2 %gather_fusion = bf16[16,4,64,256]{3,2,1,0:T(8,128)(2,1)} fusion(bf16[4,4,8,64,256]{4,3,2,1,0:T(8,128)(2,1)} %get-tuple-element.5, s32[16]{0:T(128)S(1)} %reshape.77), kind=kCustom, calls=%fused_computation | custom fusion | bytes 4194432 | tf_op jit(solution)/shard_map/gather | solution.py:257
  367.1 0.0 copy-done.6
  367.1 0.1 copy.18
  367.1 0.0 copy-done
  367.2 0.0 copy-start.2
  367.2 0.0 copy-start.3
  367.2 0.0 copy-start.1
  367.2 0.0 copy-start.7
  367.2 2.8 fusion
  370.0 0.0 copy-done.2
  370.0 0.1 constant_dynamic-slice_fusion
  370.0 0.0 copy-done.3
  370.0 0.1 iota_compare_fusion
  370.1 0.1 broadcast_compare_fusion
  370.2 0.0 copy-done.1
  370.2 0.0 copy-done.7
  370.2 2.2 multiply_reduce_fusion
  372.4 6.0 %psum.7 = f32[8]{0:T(128)S(1)} all-reduce(f32[8]{0:T(128)S(1)} %get-tuple-element.6), channel_id=1, replica_groups=mesh['grp'=2,'pair'=4,'aux'=2,'occ'=2] {'aux','occ'}, use_global_device_ids=true, to_apply=%region_2.3 | all-reduce | flops 8 | bytes 64 | tf_op jit(solution)/shard_map/psum | solution.py:278
  378.3 0.5 broadcast_multiply_fusion
  (1 shorter events, 0.0 us)
Async XLA Ops:
  0.6 366.5 %copy-start = (bf16[8,2,256,256]{3,2,1,0:T(8,128)(2,1)S(1)}, bf16[8,2,256,256]{3,2,1,0:T(8,128)(2,1)}, u32[]{:S(2)}) copy-start(bf16[8,2,256,256]{3,2,1,0:T(8,128)(2,1)} %param.14) | copy-start | bytes 6291460
  4.0 358.6 %copy-start.4 = (s32[32,2]{0,1:T(2,128)S(1)}, s32[32,2]{0,1:T(2,128)}, u32[]{:S(2)}) copy-start(s32[32,2]{0,1:T(2,128)} %param.23) | copy-start | bytes 772
  4.0 358.6 %copy-start.5 = (s32[32,2]{0,1:T(2,128)S(1)}, s32[32,2]{0,1:T(2,128)}, u32[]{:S(2)}) copy-start(s32[32,2]{0,1:T(2,128)} %param.22) | copy-start | bytes 772
  362.9 4.2 %copy-start.6 = (f32[8,2]{0,1:T(2,128)S(1)}, f32[8,2]{0,1:T(2,128)}, u32[]{:S(2)}) copy-start(f32[8,2]{0,1:T(2,128)} %param.18) | copy-start | bytes 196
  367.2 2.8 copy-start.2
  367.2 2.9 copy-start.3
  367.2 3.0 copy-start.1
  367.2 3.0 copy-start.7

commit v5 on v4

--- a/solution.py
+++ b/solution.py
@@ -72,15 +72,18 @@
     for copy in flying:
         copy.start()
     moves = []
-    for k in range(1, n_pair):
-        peer = pair_peer(k)
-        moves.append(remote(
-            df.at[:, pl.ds(peer * depth, depth), :], dfb.at[pl.ds(me * occ_rows, occ_rows)],
-            df_s.at[k], df_r.at[k], {"pair": peer},
-        ))
-        moves[-1].start()
-    own_df.start()
-    for hop in hops[1:]:
+
+    def send_df(first, count, part):
+        for k in range(1, n_pair):
+            peer = pair_peer(k)
+            moves.append(remote(
+                df.at[pl.ds(first, count), pl.ds(peer * depth, depth), :],
+                dfb.at[pl.ds(me * occ_rows + first, count)],
+                df_s.at[k, part], df_r.at[k, part], {"pair": peer},
+            ))
+            moves[-1].start()
+
+    for part, hop in enumerate(hops[1:], 1):
         for copy in flying:
             copy.wait()
         flying = doubling(hop)
@@ -98,6 +101,8 @@
     ]
     for copy in rot_g + amp_g:
         copy.start()
+    send_df(0, occ_rows, 0)
+    own_df.start()
     for copy in rot_g + amp_g:
         copy.wait()
     own_df.wait()
@@ -209,7 +214,7 @@
             pltpu.VMEM((n_pair,) + block, bf16),
             pltpu.VMEM((n_pair,) + block, bf16),
             dma((3,)),
-            dma((n_pair,)), dma((n_pair,)),
+            dma((n_pair, n_pair.bit_length())), dma((n_pair, n_pair.bit_length())),
             dma((n_pair,)), dma((n_pair,)),
             dma((n_group,)), dma((n_group,)),
             dma((n_pair,)), dma((n_pair,)),

time: 382 us -> 307 us (0.80)
  Pallas kernels: 359 us -> 286 us
    pallas_call x1, Pallas kernels: 359 us -> 286 us  [exchange_sum(): pl.pallas_call(functools.partial(exchange_kernel, sizes), out_shape=(jax....]
where the time goes in v5:
time: 307 us; the launch traced here: 306 us
  Pallas kernels  286 us (93%)
  blocking collectives  5.71 us (2%)
  other arithmetic  5.53 us (2%)
  local copies, waits for them, and re-layouts  5.28 us (2%)
    pallas_call x1, Pallas kernels, exchange_sum(): pl.pallas_call(functools.partial(exchange_kernel, sizes), out_shape=(jax....  286 us

profile of v5, /device:TPU:0, one launch (start us, length us, event | category | flops | bytes accessed | tf_op | source)
XLA Modules:
  0.0 306.1 jit_solution(10247849492463211751)
XLA Ops:
  0.6 0.0 copy-start
  0.6 0.8 multiply_add_fusion
  1.5 0.1 copy.17
  1.6 0.6 reshape.75.idx
  2.2 1.8 convert_element_type.6.amp
  4.0 0.0 copy-start.4
  4.0 0.0 copy-start.5
  4.0 286.1 %shard_map.131 = (f32[8,64,256]{2,1,0:T(8,128)}, bf16[4,4,8,64,256]{4,3,2,1,0:T(8,128)(2,1)}) custom-call(bf16[16,1024,256]{2,1,0:T(8,128)(2,1)} %df.1, bf16[4,2,256,256]{3,2,1,0:T(8,128)(2,1)} %bitcast.5, s32[64]{0:T(128)} %reshape.75.idx, bf16[8,64,256]{2,1,0:T(8,128)(2,1)} %convert_element_type.6.amp), custom_call_target="tpu_custom_call" | custom-call | flops 3221225472 | bytes 419430400 | tf_op jit(solution)/shard_map/pallas_call | solution.py:191
  290.1 0.0 copy-done.4
  290.1 0.0 copy-done.5
  290.2 0.1 fusion.5
  290.2 0.1 copy.19
  290.3 0.1 reshape.77
  290.4 0.0 copy-start.6
  290.4 4.2 %gather_fusion = bf16[16,4,64,256]{3,2,1,0:T(8,128)(2,1)} fusion(bf16[4,4,8,64,256]{4,3,2,1,0:T(8,128)(2,1)} %get-tuple-element.5, s32[16]{0:T(128)S(1)} %reshape.77), kind=kCustom, calls=%fused_computation | custom fusion | bytes 4194432 | tf_op jit(solution)/shard_map/gather | solution.py:262
  294.6 0.0 copy-done.6
  294.6 0.1 copy.18
  294.7 0.0 copy-done
  294.7 0.0 copy-start.2
  294.7 0.0 copy-start.3
  294.7 0.0 copy-start.1
  294.7 0.0 copy-start.7
  294.7 2.8 fusion
  297.5 0.0 copy-done.2
  297.5 0.1 constant_dynamic-slice_fusion
  297.6 0.0 copy-done.3
  297.6 0.1 iota_compare_fusion
  297.7 0.1 broadcast_compare_fusion
  297.7 0.0 copy-done.1
  297.7 0.0 copy-done.7
  297.8 2.2 multiply_reduce_fusion
  299.9 5.7 %psum.7 = f32[8]{0:T(128)S(1)} all-reduce(f32[8]{0:T(128)S(1)} %get-tuple-element.6), channel_id=1, replica_groups=mesh['grp'=2,'pair'=4,'aux'=2,'occ'=2] {'aux','occ'}, use_global_device_ids=true, to_apply=%region_2.3 | all-reduce | flops 8 | bytes 64 | tf_op jit(solution)/shard_map/psum | solution.py:283
  305.6 0.5 broadcast_multiply_fusion
  (1 shorter events, 0.0 us)
Async XLA Ops:
  0.6 294.1 %copy-start = (bf16[8,2,256,256]{3,2,1,0:T(8,128)(2,1)S(1)}, bf16[8,2,256,256]{3,2,1,0:T(8,128)(2,1)}, u32[]{:S(2)}) copy-start(bf16[8,2,256,256]{3,2,1,0:T(8,128)(2,1)} %param.14) | copy-start | bytes 6291460
  4.0 286.2 %copy-start.4 = (s32[32,2]{0,1:T(2,128)S(1)}, s32[32,2]{0,1:T(2,128)}, u32[]{:S(2)}) copy-start(s32[32,2]{0,1:T(2,128)} %param.23) | copy-start | bytes 772
  4.0 286.2 %copy-start.5 = (s32[32,2]{0,1:T(2,128)S(1)}, s32[32,2]{0,1:T(2,128)}, u32[]{:S(2)}) copy-start(s32[32,2]{0,1:T(2,128)} %param.22) | copy-start | bytes 772
  290.4 4.2 %copy-start.6 = (f32[8,2]{0,1:T(2,128)S(1)}, f32[8,2]{0,1:T(2,128)}, u32[]{:S(2)}) copy-start(f32[8,2]{0,1:T(2,128)} %param.18) | copy-start | bytes 196
  294.7 2.8 copy-start.2
  294.7 2.9 copy-start.3
  294.7 3.0 copy-start.1
  294.7 3.0 copy-start.7
